TPU v7x, 32 devices: a whole 2x2x4 slice. The times are simulated.
32 devices in a mesh: dp: 8 (over z, x), seq: 4 (over y, core).
Axes of the slice: x: 2, y: 2, z: 4, core: 2. Of those that a mesh axis runs over, the one named last changes fastest.
Arguments:
- hidden_in: bfloat16 [24576, 1024], P(('dp', 'seq')), may hold values from -6 to 6
- key_bias: float32 [8, 3072], P('dp', 'seq'), may hold values from -4 to 4
- w_qkv: bfloat16 [1024, 3072], P('dp'), may hold values from -0.1875 to 0.1875
- bias_q: bfloat16 [1024], P('dp'), may hold values from -3 to 3
- bias_v: bfloat16 [1024], P('dp'), may hold values from -0.75 to 0.75
- w_out: bfloat16 [1024, 1024], P('dp'), may hold values from -3 to 3
- bias_out: bfloat16 [1024], P('dp'), may hold values from -3 to 3
- gain_attn: bfloat16 [1024], P('dp'), may hold values from 0.25 to 1.75
- shift_attn: bfloat16 [1024], P('dp'), may hold values from -3 to 3
- w_up: bfloat16 [1024, 4096], P('dp'), may hold values from -0.1875 to 0.1875
- bias_up: bfloat16 [4096], P('dp'), may hold values from -3 to 3
- w_down: bfloat16 [4096, 1024], P('dp'), may hold values from -0.09375 to 0.09375
- bias_down: bfloat16 [1024], P('dp'), may hold values from -3 to 3
- gain_ffn: bfloat16 [1024], P('dp'), may hold values from 0.25 to 1.75
- shift_ffn: bfloat16 [1024], P('dp'), may hold values from -3 to 3
- grad_out: bfloat16 [24576, 1024], P(('dp', 'seq')), may hold values from -6 to 6
Outputs:
- output: bfloat16 [24576, 1024], P(('dp', 'seq'))
- grad_in: float32 [24576, 1024], P(('dp', 'seq'))
- grad_w_qkv: float32 [1024, 3072], P('dp')
- grad_bias_q: float32 [1024], P('dp')
- grad_bias_v: float32 [1024], P('dp')
- grad_w_out: float32 [1024, 1024], P('dp')
- grad_bias_out: float32 [1024], P('dp')
- grad_gain_attn: float32 [1024], P('dp')
- grad_shift_attn: float32 [1024], P('dp')
- grad_w_up: float32 [1024, 4096], P('dp')
- grad_bias_up: float32 [4096], P('dp')
- grad_w_down: float32 [4096, 1024], P('dp')
- grad_bias_down: float32 [1024], P('dp')
- grad_gain_ffn: float32 [1024], P('dp')
- grad_shift_ffn: float32 [1024], P('dp')
All inputs are finite; a program needn't handle non-finite values.
Results may differ from a plain program's by a relative error of at most 0.02.
Values may be sent and summed in bfloat16 or wider, within the bound.
A program may use at most 192 MiB of HBM per device.

v0:
```python
import jax
import jax.numpy as jnp
from jax import lax
from jax.sharding import PartitionSpec as P

HEAD_DIM = 64
norm_eps = 1e-05


def shortened(array):

    def short(part):
        return part.astype(jnp.bfloat16) if part.dtype == jnp.float32 else part

    return jax.tree.map(short, array)


def layer_norm(hidden, gain_vec, shift_vec):
    row_mean = jnp.mean(hidden, -1, keepdims=True)
    centered = hidden - row_mean
    row_var = jnp.mean(centered * centered, -1, keepdims=True)
    return centered * lax.rsqrt(row_var + norm_eps) * gain_vec + shift_vec


def gelu_exact(pre_act):
    return jax.nn.gelu(pre_act, approximate=False)


def matmul(left, right):
    return jnp.dot(left, right, preferred_element_type=jnp.float32)


def matmul_left(left, right):
    return lax.dot_general(
        left, right, (((0,), (0,)), ((), ())), preferred_element_type=jnp.float32
    )


def matmul_right(left, right):
    return lax.dot_general(
        left, right, (((1,), (1,)), ((), ())), preferred_element_type=jnp.float32
    )


def attend_forward(queries, keys_all, values_all, bias_row, score_scale):
    length, heads_loc, head_width = queries.shape
    block_rows = min(512, length)
    head_step = min(2, heads_loc)
    blocks = queries.reshape(length // block_rows, block_rows, heads_loc, head_width)

    def one_block(query_blk):
        pieces = []
        totals_list = []
        for start_head in range(0, heads_loc, head_step):
            part = slice(start_head, start_head + head_step)
            scores = (
                jnp.einsum(
                    "bhe,lhe->hbl",
                    query_blk[:, part],
                    keys_all[:, part],
                    preferred_element_type=jnp.float32,
                )
                * score_scale
                + bias_row
            )
            row_max = jnp.max(scores, -1, keepdims=True)
            expo = jnp.exp(scores - row_max)
            row_total = jnp.sum(expo, -1, keepdims=True)
            probs_low = (expo / row_total).astype(jnp.bfloat16)
            pieces.append(
                jnp.einsum(
                    "hbl,lhe->bhe",
                    probs_low,
                    values_all[:, part],
                    preferred_element_type=jnp.float32,
                )
            )
            totals_list.append((row_max + jnp.log(row_total))[..., 0])
        return (jnp.concatenate(pieces, 1).astype(jnp.bfloat16), jnp.concatenate(totals_list, 0))

    context, log_total = lax.map(one_block, blocks)
    return (context.reshape(length, heads_loc * head_width), log_total)


def attend_backward(queries, keys_all, values_all, bias_row, score_scale, log_total, context_grad):
    length, heads_loc, head_width = queries.shape
    block_rows = min(512, length)
    head_step = min(2, heads_loc)
    query_blocks = queries.reshape(length // block_rows, block_rows, heads_loc, head_width)
    grad_blocks = context_grad.reshape(length // block_rows, block_rows, heads_loc, head_width)

    def one_block(carry_in, item_in):
        key_acc, value_acc = carry_in
        query_blk, grad_blk, total_blk = item_in
        query_parts = []
        key_parts = []
        value_parts = []
        for start_head in range(0, heads_loc, head_step):
            part = slice(start_head, start_head + head_step)
            scores = (
                jnp.einsum(
                    "bhe,lhe->hbl",
                    query_blk[:, part],
                    keys_all[:, part],
                    preferred_element_type=jnp.float32,
                )
                * score_scale
                + bias_row
            )
            probs_full = jnp.exp(scores - total_blk[part][..., None])
            d_probs = jnp.einsum(
                "bhe,lhe->hbl",
                grad_blk[:, part],
                values_all[:, part],
                preferred_element_type=jnp.float32,
            )
            row_dot = jnp.sum(probs_full * d_probs, -1, keepdims=True)
            d_scores = (probs_full * (d_probs - row_dot)).astype(jnp.bfloat16)
            query_parts.append(
                jnp.einsum(
                    "hbl,lhe->bhe", d_scores, keys_all[:, part], preferred_element_type=jnp.float32
                )
                * score_scale
            )
            key_parts.append(
                jnp.einsum(
                    "hbl,bhe->lhe", d_scores, query_blk[:, part], preferred_element_type=jnp.float32
                )
                * score_scale
            )
            value_parts.append(
                jnp.einsum(
                    "hbl,bhe->lhe",
                    probs_full.astype(jnp.bfloat16),
                    grad_blk[:, part],
                    preferred_element_type=jnp.float32,
                )
            )
        key_acc = key_acc + jnp.concatenate(key_parts, 1)
        value_acc = value_acc + jnp.concatenate(value_parts, 1)
        return ((key_acc, value_acc), jnp.concatenate(query_parts, 1))

    empty = jnp.zeros((length, heads_loc, head_width), jnp.float32)
    (key_grad, value_grad), query_grad = lax.scan(
        one_block, (empty, empty), (query_blocks, grad_blocks, log_total)
    )
    return (query_grad.reshape(length, heads_loc, head_width), key_grad, value_grad)


def local(
    hidden_in,
    key_bias,
    w_qkv,
    bias_q,
    bias_v,
    w_out,
    bias_out,
    gain_attn,
    shift_attn,
    w_up,
    bias_up,
    w_down,
    bias_down,
    gain_ffn,
    shift_ffn,
    grad_out,
):
    groups = lax.axis_size("seq")
    params = (
        lax.all_gather(w_qkv, "dp", axis=0, tiled=True),
        lax.all_gather(bias_q, "dp", axis=0, tiled=True),
        lax.all_gather(bias_v, "dp", axis=0, tiled=True),
        lax.all_gather(w_out, "dp", axis=0, tiled=True),
        lax.all_gather(bias_out, "dp", axis=0, tiled=True),
        lax.all_gather(gain_attn, "dp", axis=0, tiled=True),
        lax.all_gather(shift_attn, "dp", axis=0, tiled=True),
        lax.all_gather(w_up, "dp", axis=0, tiled=True),
        lax.all_gather(bias_up, "dp", axis=0, tiled=True),
        lax.all_gather(w_down, "dp", axis=0, tiled=True),
        lax.all_gather(bias_down, "dp", axis=0, tiled=True),
        lax.all_gather(gain_ffn, "dp", axis=0, tiled=True),
        lax.all_gather(shift_ffn, "dp", axis=0, tiled=True),
    )
    full_bias_q = params[1].astype(jnp.float32)
    full_bias_v = params[2].astype(jnp.float32)
    full_bias_out = params[4].astype(jnp.float32)
    full_gain_attn = params[5].astype(jnp.float32)
    full_shift_attn = params[6].astype(jnp.float32)
    full_bias_up = params[8].astype(jnp.float32)
    full_bias_down = params[10].astype(jnp.float32)
    full_gain_ffn = params[11].astype(jnp.float32)
    full_shift_ffn = params[12].astype(jnp.float32)
    tok_rows, model_width = hidden_in.shape
    group_width = model_width // groups
    heads_loc = group_width // HEAD_DIM
    score_scale = HEAD_DIM ** (-0.5)
    no_bias = jnp.zeros((model_width,), jnp.float32)
    qkv_rows = matmul(hidden_in, params[0]) + jnp.concatenate([full_bias_q, no_bias, full_bias_v])
    qkv_rows = qkv_rows.astype(jnp.bfloat16).reshape(tok_rows, 3, groups, group_width)
    heads_in = lax.all_to_all(qkv_rows, "seq", split_axis=2, concat_axis=0, tiled=True)
    length = heads_in.shape[0]
    queries = heads_in[:, 0, 0].reshape(length, heads_loc, HEAD_DIM)
    keys_all = heads_in[:, 1, 0].reshape(length, heads_loc, HEAD_DIM)
    values_all = heads_in[:, 2, 0].reshape(length, heads_loc, HEAD_DIM)
    bias_row = lax.all_gather(key_bias, "seq", axis=1, tiled=True)[0]
    context_heads, log_total = attend_forward(queries, keys_all, values_all, bias_row, score_scale)
    context = lax.all_to_all(
        shortened(context_heads.reshape(length, 1, group_width)),
        "seq",
        split_axis=0,
        concat_axis=1,
        tiled=True,
    ).reshape(tok_rows, model_width)
    attended = hidden_in.astype(jnp.float32) + matmul(context, params[3]) + full_bias_out
    normed = layer_norm(attended, full_gain_attn, full_shift_attn)
    normed_low = normed.astype(jnp.bfloat16)
    pre_act = matmul(normed_low, params[7]) + full_bias_up
    activ = gelu_exact(pre_act).astype(jnp.bfloat16)
    branch_sum = normed + matmul(activ, params[9]) + full_bias_down
    output = layer_norm(branch_sum, full_gain_ffn, full_shift_ffn).astype(jnp.bfloat16)
    matrices = (
        lax.all_gather(w_qkv, "dp", axis=0, tiled=True),
        lax.all_gather(w_out, "dp", axis=0, tiled=True),
        lax.all_gather(w_up, "dp", axis=0, tiled=True),
        lax.all_gather(w_down, "dp", axis=0, tiled=True),
    )
    upstream = grad_out.astype(jnp.float32)
    _, norm_back = jax.vjp(layer_norm, branch_sum, full_gain_ffn, full_shift_ffn)
    d_branch, grad_gain_ffn, grad_shift_ffn = norm_back(upstream)
    grad_bias_down = jnp.sum(d_branch, 0)
    d_branch_low = d_branch.astype(jnp.bfloat16)
    grad_w_down = matmul_left(activ, d_branch_low)
    d_activ = matmul_right(d_branch_low, matrices[3])
    _, gelu_back = jax.vjp(gelu_exact, pre_act)
    d_pre = gelu_back(d_activ)[0]
    grad_bias_up = jnp.sum(d_pre, 0)
    d_pre_low = d_pre.astype(jnp.bfloat16)
    grad_w_up = matmul_left(normed_low, d_pre_low)
    d_normed = d_branch + matmul_right(d_pre_low, matrices[2])
    _, attn_norm_back = jax.vjp(layer_norm, attended, full_gain_attn, full_shift_attn)
    d_attended, grad_gain_attn, grad_shift_attn = attn_norm_back(d_normed)
    grad_bias_out = jnp.sum(d_attended, 0)
    d_attended_low = d_attended.astype(jnp.bfloat16)
    grad_w_out = matmul_left(context, d_attended_low)
    d_context = matmul_right(d_attended_low, matrices[1]).astype(jnp.bfloat16)
    d_context_heads = lax.all_to_all(
        d_context.reshape(tok_rows, groups, group_width),
        "seq",
        split_axis=1,
        concat_axis=0,
        tiled=True,
    )
    query_grad, key_grad, value_grad = attend_backward(
        queries,
        keys_all,
        values_all,
        bias_row,
        score_scale,
        log_total,
        d_context_heads.reshape(length, heads_loc, HEAD_DIM),
    )
    d_heads = (
        jnp.stack([query_grad, key_grad, value_grad], 1)
        .astype(jnp.bfloat16)
        .reshape(length, 3, 1, group_width)
    )
    d_qkv = lax.all_to_all(d_heads, "seq", split_axis=0, concat_axis=2, tiled=True).reshape(
        tok_rows, 3 * model_width
    )
    grad_bias_q = jnp.sum(d_qkv[:, :model_width].astype(jnp.float32), 0)
    grad_bias_v = jnp.sum(d_qkv[:, 2 * model_width :].astype(jnp.float32), 0)
    grad_w_qkv = matmul_left(hidden_in, d_qkv)
    grad_in = d_attended + matmul_right(d_qkv, matrices[0])
    local_grads = (
        grad_w_qkv,
        grad_bias_q,
        grad_bias_v,
        grad_w_out,
        grad_bias_out,
        grad_gain_attn,
        grad_shift_attn,
        grad_w_up,
        grad_bias_up,
        grad_w_down,
        grad_bias_down,
        grad_gain_ffn,
        grad_shift_ffn,
    )
    shares = (
        lax.psum_scatter(
            local_grads[0].astype(jnp.bfloat16), "dp", scatter_dimension=0, tiled=True
        ).astype(jnp.float32),
        lax.psum_scatter(
            local_grads[1].astype(jnp.bfloat16), "dp", scatter_dimension=0, tiled=True
        ).astype(jnp.float32),
        lax.psum_scatter(
            local_grads[2].astype(jnp.bfloat16), "dp", scatter_dimension=0, tiled=True
        ).astype(jnp.float32),
        lax.psum_scatter(
            local_grads[3].astype(jnp.bfloat16), "dp", scatter_dimension=0, tiled=True
        ).astype(jnp.float32),
        lax.psum_scatter(
            local_grads[4].astype(jnp.bfloat16), "dp", scatter_dimension=0, tiled=True
        ).astype(jnp.float32),
        lax.psum_scatter(
            local_grads[5].astype(jnp.bfloat16), "dp", scatter_dimension=0, tiled=True
        ).astype(jnp.float32),
        lax.psum_scatter(
            local_grads[6].astype(jnp.bfloat16), "dp", scatter_dimension=0, tiled=True
        ).astype(jnp.float32),
        lax.psum_scatter(
            local_grads[7].astype(jnp.bfloat16), "dp", scatter_dimension=0, tiled=True
        ).astype(jnp.float32),
        lax.psum_scatter(
            local_grads[8].astype(jnp.bfloat16), "dp", scatter_dimension=0, tiled=True
        ).astype(jnp.float32),
        lax.psum_scatter(
            local_grads[9].astype(jnp.bfloat16), "dp", scatter_dimension=0, tiled=True
        ).astype(jnp.float32),
        lax.psum_scatter(
            local_grads[10].astype(jnp.bfloat16), "dp", scatter_dimension=0, tiled=True
        ).astype(jnp.float32),
        lax.psum_scatter(
            local_grads[11].astype(jnp.bfloat16), "dp", scatter_dimension=0, tiled=True
        ).astype(jnp.float32),
        lax.psum_scatter(
            local_grads[12].astype(jnp.bfloat16), "dp", scatter_dimension=0, tiled=True
        ).astype(jnp.float32),
    )
    owned_grads = (
        lax.psum(shares[0].astype(jnp.bfloat16), "seq").astype(jnp.float32),
        lax.psum(shares[1].astype(jnp.bfloat16), "seq").astype(jnp.float32),
        lax.psum(shares[2].astype(jnp.bfloat16), "seq").astype(jnp.float32),
        lax.psum(shares[3].astype(jnp.bfloat16), "seq").astype(jnp.float32),
        lax.psum(shares[4].astype(jnp.bfloat16), "seq").astype(jnp.float32),
        lax.psum(shares[5].astype(jnp.bfloat16), "seq").astype(jnp.float32),
        lax.psum(shares[6].astype(jnp.bfloat16), "seq").astype(jnp.float32),
        lax.psum(shares[7].astype(jnp.bfloat16), "seq").astype(jnp.float32),
        lax.psum(shares[8].astype(jnp.bfloat16), "seq").astype(jnp.float32),
        lax.psum(shares[9].astype(jnp.bfloat16), "seq").astype(jnp.float32),
        lax.psum(shares[10].astype(jnp.bfloat16), "seq").astype(jnp.float32),
        lax.psum(shares[11].astype(jnp.bfloat16), "seq").astype(jnp.float32),
        lax.psum(shares[12].astype(jnp.bfloat16), "seq").astype(jnp.float32),
    )
    return (
        output,
        grad_in,
        owned_grads[0],
        owned_grads[1],
        owned_grads[2],
        owned_grads[3],
        owned_grads[4],
        owned_grads[5],
        owned_grads[6],
        owned_grads[7],
        owned_grads[8],
        owned_grads[9],
        owned_grads[10],
        owned_grads[11],
        owned_grads[12],
    )


def solution(mesh):
    return jax.shard_map(
        local,
        mesh=mesh,
        in_specs=(
            P(("dp", "seq"), None),
            P("dp", "seq"),
            P("dp", None),
            P("dp"),
            P("dp"),
            P("dp", None),
            P("dp"),
            P("dp"),
            P("dp"),
            P("dp", None),
            P("dp"),
            P("dp", None),
            P("dp"),
            P("dp"),
            P("dp"),
            P(("dp", "seq"), None),
        ),
        out_specs=(
            P(("dp", "seq"), None),
            P(("dp", "seq"), None),
            P("dp", None),
            P("dp"),
            P("dp"),
            P("dp", None),
            P("dp"),
            P("dp"),
            P("dp"),
            P("dp", None),
            P("dp"),
            P("dp", None),
            P("dp"),
            P("dp"),
            P("dp"),
        ),
        check_vma=False,
    )
```

profile of v0, /device:TPU:0, one launch (start us, length us, event | category | flops | bytes accessed | tf_op | source)
XLA Modules:
  0.0 1988.5 jit_solution(5152587531738367793)
XLA Ops:
  9.4 22.5 %all-gather.1 = bf16[8,1,128]{2,1,0:T(2,128)(2,1)S(1)} all-gather(bf16[1,1,128]{2,1,0:T(2,128)(2,1)} %bitcast.231), channel_id=1, replica_groups=mesh['dp'=8,'seq'=4] {'dp'}, dimensions={0}, use_global_device_ids=true | all-gather | bytes 2304 | tf_op jit(solution)/shard_map/all_gather | solution.py:172
  31.9 16.7 all-gather
  48.6 63.4 %all-gather.14.cloned.1.call-done = bf16[1024,3072]{1,0:T(8,128)(2,1)} async-done(((bf16[128,3072]{1,0:T(8,128)(2,1)}), bf16[1024,3072]{1,0:T(8,128)(2,1)}) %all-gather.14.cloned.1.call-update) | async-done | bytes 6291472 | tf_op jit(solution)/shard_map/all_gather | solution.py:170
  112.0 9.1 add_convert_fusion
  121.1 9.7 reshape.215
  141.7 54.1 %all_gather.49 = f32[1,3072]{1,0:T(1,128)S(1)} all-gather(f32[1,768]{1,0:T(1,128)S(1)} %copy-done.34), channel_id=1, replica_groups=mesh['dp'=8,'seq'=4] {'seq'}, dimensions={1}, use_global_device_ids=true | all-gather | bytes 15360 | tf_op jit(solution)/shard_map/all_gather | solution.py:205
  213.4 180.6 %while.27 = (s32[]{:T(128)}, bf16[6,512,4,64]{1,3,2,0:T(8,128)(2,1)}, f32[6,4,512]{2,1,0:T(4,128)S(1)}, bf16[6,512,4,64]{1,3,2,0:T(8,128)(2,1)}, bf16[3072,4,64]...) while((s32[]{:T(128)}, bf16[6,512,4,64]{1,3,2,0:T(8,128)(2,1)}, ...), condition=%wide.region_5.6_spmd, body=%wide.region_0.5_spmd.sunk | while | flops 1686765568 | bytes 80098904 | solution.py:81
  221.0 7.9 fusion.168
  250.8 7.9 fusion.168
  280.9 7.9 fusion.168
  311.3 7.9 fusion.168
  333.6 8.2 fusion.167
  341.9 7.9 fusion.168
  371.7 7.9 fusion.168
  399.7 22.8 %reshape.246 = bf16[3072,1,256]{2,1,0:T(2,128)(2,1)} reshape(bf16[6,512,4,64]{3,2,1,0:T(4,128)(2,1)} %copy.114) | data formatting | bytes 3145728 | tf_op jit(solution)/shard_map/reshape;reshape | solution.py:208
  423.0 16.7 reduce.3
  445.9 17.5 all-gather.2
  463.3 16.9 all-gather.3
  480.2 17.5 all-gather.4
  497.7 26.0 %all-gather.5 = bf16[8,1,512]{2,1,0:T(2,128)(2,1)S(1)} all-gather(bf16[1,1,512]{2,1,0:T(2,128)(2,1)S(1)} %reshape.229), channel_id=1, replica_groups=mesh['dp'=8,'seq'=4] {'dp'}, dimensions={0}, use_global_device_ids=true | all-gather | bytes 9216 | tf_op jit(solution)/shard_map/all_gather | solution.py:178
  523.8 16.2 all-gather.6
  539.9 18.2 all-gather.7
  558.1 16.2 all-gather.8
  586.4 39.4 %multiply_convert_fusion.2 = (bf16[768,4096]{1,0:T(8,128)(2,1)}, f32[768,4096]{1,0:T(8,128)}, f32[768,4096]{1,0:T(8,128)}) fusion(f32[4096]{0:T(1024)S(1)} %bitcast.222, bf16[1024,4096]{1,0:T(8,128)(2,1)} %all-gather.18.cloned.1.call-done, f32[768,1024]{1,0:T(8,128)S(1)} %get-tuple-element.410, f32[1024]{0:T(1024)S(1)} %bitcast.226, ...), kind=kOutput, calls=%fused_computation.100 | convolution fusion | flops 6654001152 | bytes 43022336 | tf_op jit(solution)/shard_map/dot_general | solution.py:30
  625.8 11.7 fusion.105
  642.8 21.7 %fusion.106 = (bf16[4096]{0:T(1024)(128)(2,1)}, bf16[768,4096]{1,0:T(8,128)(2,1)}) fusion(f32[768,4096]{1,0:T(8,128)} %get-tuple-element.392, bf16[4096,1024]{1,0:T(8,128)(2,1)} %all-gather.20.cloned.1.call-done, f32[768,1024]{1,0:T(8,128)} %get-tuple-element.390, f32[768]{0:T(1024)S(1)} %negate_multiply_fusion.2, f32[768,4096]{1,0:T(8,128)} %get-tuple-element.411, ...), kind=kOutput, calls=%fused_computation.167 | convolution fusion | flops 6494351360 | bytes 43019264 | tf_op jit(solution)/shard_map/dot_general | solution.py:40
  664.5 13.4 multiply_reduce_fusion.2
  687.8 20.0 %all-to-all-done.2 = bf16[768,4,256]{0,2,1:T(8,128)(2,1)S(1)} async-done(((bf16[768,4,256]{0,2,1:T(8,128)(2,1)}), bf16[768,4,256]{0,2,1:T(8,128)(2,1)S(1)}, u32[]{:S(2)}, u32[]{:S(2)}) %all-to-all-start.2) | async-done | bytes 1572896 | tf_op jit(solution)/shard_map/all_to_all | solution.py:246
  717.6 568.6 %while.28 = (s32[]{:T(128)}, f32[3072,4,64]{0,2,1:T(8,128)}, f32[3072,4,64]{0,2,1:T(8,128)}, bf16[6,512,4,64]{1,3,2,0:T(8,128)(2,1)}, bf16[6,512,4,64]{1,3,2,0:T...) while((s32[]{:T(128)}, f32[3072,4,64]{0,2,1:T(8,128)}, ...), condition=%wide.region_17.18_spmd.clone, body=%wide.region_14.17_spmd.clone.sunk | while | flops 4127193088 | bytes 341160832 | solution.py:144
  732.3 7.7 fusion.192
  740.8 20.1 %multiply_reduce_fusion.7 = (f32[2,512]{1,0:T(2,128)S(1)}, f32[2,512]{1,0:T(2,128)S(1)}, f32[2,512,3072]{2,1,0:T(8,128)}) fusion(f32[2,512,3072]{2,1,0:T(8,128)} %fusion.191, f32[2,512]{1,0:T(2,128)S(1)} %get-tuple-element.546, f32[3072]{0:T(1024)S(1)} %bitcast.204, f32[2,512,3072]{2,1,0:T(8,128)} %fusion.192, f32[2,512]{1,0:T(2,128)S(1)} %get-tuple-element.547, ...), kind=kOutput, calls=%fused_computation.39.clone.1 | convolution fusion | flops 434108416 | bytes 51409408 | tf_op jit(solution)/shard_map/while/body/eval_jaxpr/bhe,lhe->hbl/dot_general | solution.py:111
  760.9 17.9 multiply_convert_fusion.4
  834.0 20.1 %multiply_reduce_fusion.7 = (f32[2,512]{1,0:T(2,128)S(1)}, f32[2,512]{1,0:T(2,128)S(1)}, f32[2,512,3072]{2,1,0:T(8,128)}) fusion(f32[2,512,3072]{2,1,0:T(8,128)} %fusion.191, f32[2,512]{1,0:T(2,128)S(1)} %get-tuple-element.546, f32[3072]{0:T(1024)S(1)} %bitcast.204, f32[2,512,3072]{2,1,0:T(8,128)} %fusion.192, f32[2,512]{1,0:T(2,128)S(1)} %get-tuple-element.547, ...), kind=kOutput, calls=%fused_computation.39.clone.1 | convolution fusion | flops 434108416 | bytes 51409408 | tf_op jit(solution)/shard_map/while/body/eval_jaxpr/bhe,lhe->hbl/dot_general | solution.py:111
  854.0 17.9 multiply_convert_fusion.4
  897.1 8.8 maximum_add_fusion.3
  920.5 7.7 fusion.192
  928.9 20.0 %multiply_reduce_fusion.7 = (f32[2,512]{1,0:T(2,128)S(1)}, f32[2,512]{1,0:T(2,128)S(1)}, f32[2,512,3072]{2,1,0:T(8,128)}) fusion(f32[2,512,3072]{2,1,0:T(8,128)} %fusion.191, f32[2,512]{1,0:T(2,128)S(1)} %get-tuple-element.546, f32[3072]{0:T(1024)S(1)} %bitcast.204, f32[2,512,3072]{2,1,0:T(8,128)} %fusion.192, f32[2,512]{1,0:T(2,128)S(1)} %get-tuple-element.547, ...), kind=kOutput, calls=%fused_computation.39.clone.1 | convolution fusion | flops 434108416 | bytes 51409408 | tf_op jit(solution)/shard_map/while/body/eval_jaxpr/bhe,lhe->hbl/dot_general | solution.py:111
  948.9 17.9 multiply_convert_fusion.4
  992.0 8.8 maximum_add_fusion.3
  1015.4 7.7 fusion.192
  1023.8 20.1 %multiply_reduce_fusion.7 = (f32[2,512]{1,0:T(2,128)S(1)}, f32[2,512]{1,0:T(2,128)S(1)}, f32[2,512,3072]{2,1,0:T(8,128)}) fusion(f32[2,512,3072]{2,1,0:T(8,128)} %fusion.191, f32[2,512]{1,0:T(2,128)S(1)} %get-tuple-element.546, f32[3072]{0:T(1024)S(1)} %bitcast.204, f32[2,512,3072]{2,1,0:T(8,128)} %fusion.192, f32[2,512]{1,0:T(2,128)S(1)} %get-tuple-element.547, ...), kind=kOutput, calls=%fused_computation.39.clone.1 | convolution fusion | flops 434108416 | bytes 51409408 | tf_op jit(solution)/shard_map/while/body/eval_jaxpr/bhe,lhe->hbl/dot_general | solution.py:111
  1043.9 17.9 multiply_convert_fusion.4
  1087.1 8.8 maximum_add_fusion.3
  1110.4 7.7 fusion.192
  1118.9 20.0 %multiply_reduce_fusion.7 = (f32[2,512]{1,0:T(2,128)S(1)}, f32[2,512]{1,0:T(2,128)S(1)}, f32[2,512,3072]{2,1,0:T(8,128)}) fusion(f32[2,512,3072]{2,1,0:T(8,128)} %fusion.191, f32[2,512]{1,0:T(2,128)S(1)} %get-tuple-element.546, f32[3072]{0:T(1024)S(1)} %bitcast.204, f32[2,512,3072]{2,1,0:T(8,128)} %fusion.192, f32[2,512]{1,0:T(2,128)S(1)} %get-tuple-element.547, ...), kind=kOutput, calls=%fused_computation.39.clone.1 | convolution fusion | flops 434108416 | bytes 51409408 | tf_op jit(solution)/shard_map/while/body/eval_jaxpr/bhe,lhe->hbl/dot_general | solution.py:111
  1138.9 17.9 multiply_convert_fusion.4
  1182.0 8.8 maximum_add_fusion.3
  1205.3 7.7 fusion.192
  1213.8 20.1 %multiply_reduce_fusion.7 = (f32[2,512]{1,0:T(2,128)S(1)}, f32[2,512]{1,0:T(2,128)S(1)}, f32[2,512,3072]{2,1,0:T(8,128)}) fusion(f32[2,512,3072]{2,1,0:T(8,128)} %fusion.191, f32[2,512]{1,0:T(2,128)S(1)} %get-tuple-element.546, f32[3072]{0:T(1024)S(1)} %bitcast.204, f32[2,512,3072]{2,1,0:T(8,128)} %fusion.192, f32[2,512]{1,0:T(2,128)S(1)} %get-tuple-element.547, ...), kind=kOutput, calls=%fused_computation.39.clone.1 | convolution fusion | flops 434108416 | bytes 51409408 | tf_op jit(solution)/shard_map/while/body/eval_jaxpr/bhe,lhe->hbl/dot_general | solution.py:111
  1233.9 17.9 multiply_convert_fusion.4
  1277.1 8.8 maximum_add_fusion.3
  1299.2 10.1 copy.110
  1309.3 74.6 %all_to_all.63 = bf16[3072,3,1,256]{3,1,2,0:T(4,128)(2,1)S(1)} all-to-all(bf16[3072,3,1,256]{3,1,2,0:T(4,128)(2,1)} %copy.110), channel_id=1, replica_groups=mesh['dp'=8,'seq'=4] {'seq'}, dimensions={0} | all-to-all | bytes 9437184 | tf_op jit(solution)/shard_map/all_to_all | solution.py:267
  1393.5 9.3 convert_bitcast_fusion
  1402.9 8.7 copy.116
  1418.1 12.5 convolution_convert_fusion
  1432.6 12.3 convolution_convert_fusion.1
  1453.9 36.6 %all-reduce.9 = (bf16[1024]{0:T(1024)(128)(2,1)S(1)}, bf16[1024]{0:T(1024)(128)(2,1)S(1)}, bf16[1024]{0:T(1024)(128)(2,1)S(1)}, bf16[1024]{0:T(1024)(128)(2,1)S(...) all-reduce(bf16[1024]{0:T(1024)(128)(2,1)S(1)} %get-tuple-element.3, ...), channel_id=3, replica_groups=mesh['dp'=8,'seq'=4] {'dp'}, use_global_device_ids=true, to_apply=%region_21.22.clone | all-reduce | flops 12288 | bytes 49152
  1501.6 26.6 %reduce-scatter.13.cloned.1.call-done = bf16[128,3072]{1,0:T(8,128)(2,1)} async-done(((bf16[1024,3072]{1,0:T(8,128)(2,1)}), bf16[128,3072]{1,0:T(8,128)(2,1)}) %reduce-scatter.13.cloned.1.call-update) | async-done | bytes 786448
  1530.4 68.5 %reduce-scatter.7.cloned.1.call-done = bf16[128,1024]{1,0:T(8,128)(2,1)} async-done(((bf16[1024,1024]{1,0:T(8,128)(2,1)}), bf16[128,1024]{1,0:T(8,128)(2,1)}) %reduce-scatter.7.cloned.1.call-update) | async-done | bytes 262160 | tf_op jit(solution)/shard_map/reduce_scatter | solution.py:299
  1598.9 151.6 %reduce-scatter.11.cloned.1.call-done = bf16[512,1024]{1,0:T(8,128)(2,1)} async-done(((bf16[4096,1024]{1,0:T(8,128)(2,1)}), bf16[512,1024]{1,0:T(8,128)(2,1)}) %reduce-scatter.11.cloned.1.call-update) | async-done | bytes 1048592 | tf_op jit(solution)/shard_map/reduce_scatter | solution.py:317
  1750.6 152.1 %reduce-scatter.9.cloned.1.call-done = bf16[128,4096]{1,0:T(8,128)(2,1)} async-done(((bf16[1024,4096]{1,0:T(8,128)(2,1)}), bf16[128,4096]{1,0:T(8,128)(2,1)}) %reduce-scatter.9.cloned.1.call-update) | async-done | bytes 1048592 | tf_op jit(solution)/shard_map/reduce_scatter | solution.py:311
  1902.7 9.8 add_add_fusion.4
  1912.6 61.3 %all-reduce.14.cloned.1.call-done = (bf16[128,3072]{0,1:T(8,128)(2,1)}, bf16[128,1024]{1,0:T(8,128)(2,1)}, bf16[128,4096]{1,0:T(8,128)(2,1)}, bf16[512,1024]{1,0:T(8,128)(2,1)}) async-done(((bf16[128,3072]{0,1:T(8,128)(2,1)}, bf16[128,1024]{1,0:T(8,128)(2,1)}, bf16[128,4096]{1,0:T(8,128)(2,1)}, bf16[512,1024]{1,0:T(8,128)(2,1)}), (bf16[128,3072]{0,1:T(8,128)(2,1)}, bf16[128,1024]{1,0:T(8,128)(2,1)}, ...) | async-done | bytes 3145744 | tf_op jit(solution)/shard_map/psum | solution.py:331
  (413 shorter events, 521.8 us)
Async XLA Ops:
  7.2 104.8 %all-gather.14.cloned.1.call-start = ((), (), s32[]{:S(2)}) async-start(), calls=%async_computation.8 | async-start | bytes 7077888 | tf_op jit(solution)/shard_map/all_gather | solution.py:170
  7.9 573.4 %all-gather.16.cloned.1.call-start = ((), (), s32[]{:S(2)}) async-start(), calls=%async_computation.9 | async-start | bytes 2359296 | tf_op jit(solution)/shard_map/all_gather | solution.py:173
  8.7 577.7 %all-gather.18.cloned.1.call-start = ((), (), s32[]{:S(2)}) async-start(), calls=%async_computation.10 | async-start | bytes 9437184 | tf_op jit(solution)/shard_map/all_gather | solution.py:177
  135.9 59.9 %all-to-all-start = ((bf16[768,3,4,256]{3,0,1,2:T(8,128)(2,1)}), bf16[768,3,4,256]{3,0,1,2:T(8,128)(2,1)}, u32[]{:S(2)}, u32[]{:S(2)}) async-start(bf16[768,3,4,256]{3,0,1,2:T(8,128)(2,1)} %copy.96), calls=%async_computation | async-start | bytes 9437184 | tf_op jit(solution)/shard_map/all_to_all | solution.py:200
  141.1 484.7 %all-gather.20.cloned.1.call-start = ((), (), s32[]{:S(2)}) async-start(), calls=%async_computation.11 | async-start | bytes 9437184 | tf_op jit(solution)/shard_map/all_gather | solution.py:179
  394.0 28.4 %copy-start.1 = (bf16[3072,4,64]{0,2,1:T(8,128)(2,1)}, bf16[3072,4,64]{0,2,1:T(8,128)(2,1)S(1)}, u32[]{:S(2)}) copy-start(bf16[3072,4,64]{0,2,1:T(8,128)(2,1)S(1)} %get-tuple-element.634) | copy-start | bytes 4718596
  394.0 28.4 %copy-start.14 = (f32[1,3072]{1,0:T(1,128)}, f32[1,3072]{1,0:T(1,128)S(1)}, u32[]{:S(2)}) copy-start(f32[1,3072]{1,0:T(1,128)S(1)} %get-tuple-element.653) | copy-start | bytes 36868
  394.0 28.4 %copy-start.21 = (f32[6,4,512]{2,1,0:T(4,128)}, f32[6,4,512]{2,1,0:T(4,128)S(1)}, u32[]{:S(2)}) copy-start(f32[6,4,512]{2,1,0:T(4,128)S(1)} %get-tuple-element.586) | copy-start | bytes 147460
  422.9 22.9 %copy-start.38 = (bf16[128]{0:T(256)(128)(2,1)S(1)}, bf16[128]{0:T(256)(128)(2,1)}, u32[]{:S(2)}) copy-start(bf16[128]{0:T(256)(128)(2,1)} %param.26) | copy-start | bytes 772
  422.9 40.4 %copy-start.39 = (bf16[128]{0:T(256)(128)(2,1)S(1)}, bf16[128]{0:T(256)(128)(2,1)}, u32[]{:S(2)}) copy-start(bf16[128]{0:T(256)(128)(2,1)} %param.27) | copy-start | bytes 772
  422.9 57.3 %copy-start.40 = (bf16[128]{0:T(256)(128)(2,1)S(1)}, bf16[128]{0:T(256)(128)(2,1)}, u32[]{:S(2)}) copy-start(bf16[128]{0:T(256)(128)(2,1)} %param.28) | copy-start | bytes 772
  422.9 74.8 %copy-start.37 = (bf16[512]{0:T(512)(128)(2,1)S(1)}, bf16[512]{0:T(512)(128)(2,1)}, u32[]{:S(2)}) copy-start(bf16[512]{0:T(512)(128)(2,1)} %param.30) | copy-start | bytes 3076
  422.9 100.8 %copy-start.41 = (bf16[128]{0:T(256)(128)(2,1)S(1)}, bf16[128]{0:T(256)(128)(2,1)}, u32[]{:S(2)}) copy-start(bf16[128]{0:T(256)(128)(2,1)} %param.32) | copy-start | bytes 772
  423.0 117.0 %copy-start.42 = (bf16[128]{0:T(256)(128)(2,1)S(1)}, bf16[128]{0:T(256)(128)(2,1)}, u32[]{:S(2)}) copy-start(bf16[128]{0:T(256)(128)(2,1)} %param.33) | copy-start | bytes 772
  423.0 135.1 %copy-start.43 = (bf16[128]{0:T(256)(128)(2,1)S(1)}, bf16[128]{0:T(256)(128)(2,1)}, u32[]{:S(2)}) copy-start(bf16[128]{0:T(256)(128)(2,1)} %param.34) | copy-start | bytes 772
  441.5 132.8 %all-to-all-start.1 = ((bf16[4,2,98304]{2,1,0:T(2,128)(2,1)}), bf16[4,2,98304]{2,1,0:T(2,128)(2,1)}, u32[]{:S(2)}, u32[]{:S(2)}) async-start(bf16[4,2,98304]{2,1,0:T(2,128)(2,1)} %reshape.259), calls=%async_computation.1 | async-start | bytes 3145728 | tf_op jit(solution)/shard_map/all_to_all | solution.py:207
  480.2 197.7 %copy-start.24 = (f32[8,1,128]{2,1,0:T(1,128)}, f32[8,1,128]{2,1,0:T(1,128)S(1)}, u32[]{:S(2)}) copy-start(f32[8,1,128]{2,1,0:T(1,128)S(1)} %convert_element_type.240) | copy-start | bytes 12292
  497.7 128.1 %copy-start.32 = (f32[8,1,128]{2,1,0:T(1,128)}, f32[8,1,128]{2,1,0:T(1,128)S(1)}, u32[]{:S(2)}) copy-start(f32[8,1,128]{2,1,0:T(1,128)S(1)} %convert_element_type.241) | copy-start | bytes 12292
  585.9 92.1 %copy-start.8 = (f32[768,1024]{1,0:T(8,128)}, f32[768,1024]{1,0:T(8,128)S(1)}, u32[]{:S(2)}) copy-start(f32[768,1024]{1,0:T(8,128)S(1)} %get-tuple-element.410) | copy-start | bytes 9437188
  585.9 92.1 %copy-start.19 = (f32[768]{0:T(1024)}, f32[768]{0:T(1024)S(1)}, u32[]{:S(2)}) copy-start(f32[768]{0:T(1024)S(1)} %broadcast_multiply_fusion.1) | copy-start | bytes 9220
  586.4 91.6 %copy-start.26 = (f32[768]{0:T(1024)}, f32[768]{0:T(1024)S(1)}, u32[]{:S(2)}) copy-start(f32[768]{0:T(1024)S(1)} %fusion.94) | copy-start | bytes 9220
  625.8 12.2 copy-start.6
  642.8 21.7 %copy-start.28 = (f32[768]{0:T(1024)}, f32[768]{0:T(1024)S(1)}, u32[]{:S(2)}) copy-start(f32[768]{0:T(1024)S(1)} %negate_multiply_fusion.2) | copy-start | bytes 9220
  684.1 23.6 %all-to-all-start.2 = ((bf16[768,4,256]{0,2,1:T(8,128)(2,1)}), bf16[768,4,256]{0,2,1:T(8,128)(2,1)S(1)}, u32[]{:S(2)}, u32[]{:S(2)}) async-start(bf16[768,4,256]{0,2,1:T(8,128)(2,1)} %bitcast.33), calls=%async_computation.2 | async-start | bytes 3145728 | tf_op jit(solution)/shard_map/all_to_all | solution.py:246
  687.7 840.5 %reduce-scatter.13.cloned.1.call-start = ((), (), s32[]{:S(2)}) async-start(), calls=%async_computation.15 | async-start | bytes 7077888
  707.7 9.8 copy-start.2
  707.8 9.8 copy-start.15
  778.8 15.6 slice-start.3
  782.7 11.7 slice-start.4
  786.8 7.6 slice-start.5
  791.0 8.3 slice-start
  871.9 7.2 copy-start
  871.9 15.6 slice-start.3
  875.8 11.7 slice-start.4
  879.9 7.6 slice-start.5
  884.1 8.3 slice-start
  897.1 8.8 copy-start.3
  966.8 15.6 slice-start.3
  970.7 11.7 slice-start.4
  974.8 7.6 slice-start.5
  979.0 8.3 slice-start
  992.0 8.8 copy-start.3
  1061.8 7.2 copy-start
  1061.8 15.6 slice-start.3
  1065.7 11.7 slice-start.4
  1069.8 7.6 slice-start.5
  1074.0 8.3 slice-start
  1087.1 8.8 copy-start.3
  1156.8 15.6 slice-start.3
  1160.7 11.7 slice-start.4
  1164.7 7.6 slice-start.5
  1168.9 8.3 slice-start
  1182.0 8.8 copy-start.3
  1251.8 15.6 slice-start.3
  1255.7 11.7 slice-start.4
  1259.8 7.6 slice-start.5
  1264.0 8.3 slice-start
  1277.1 8.8 copy-start.3
  1286.2 8.2 copy-start.4
  1411.6 187.3 %reduce-scatter.7.cloned.1.call-start = ((), (), s32[]{:S(2)}) async-start(), calls=%async_computation.12 | async-start | bytes 2359296 | tf_op jit(solution)/shard_map/reduce_scatter | solution.py:299
  1418.0 332.5 %reduce-scatter.11.cloned.1.call-start = ((), (), s32[]{:S(2)}) async-start(), calls=%async_computation.14 | async-start | bytes 9437184 | tf_op jit(solution)/shard_map/reduce_scatter | solution.py:317
  1430.6 472.1 %reduce-scatter.9.cloned.1.call-start = ((), (), s32[]{:S(2)}) async-start(), calls=%async_computation.13 | async-start | bytes 9437184 | tf_op jit(solution)/shard_map/reduce_scatter | solution.py:311
  1444.9 529.0 %all-reduce.14.cloned.1.call-start = ((), (), s32[]{:S(2)}) async-start(), calls=%async_computation.16 | async-start | bytes 6291456 | tf_op jit(solution)/shard_map/psum | solution.py:331
  1451.3 451.4 %copy-start.12 = (f32[768,1024]{1,0:T(8,128)S(1)}, f32[768,1024]{1,0:T(8,128)}, u32[]{:S(2)}) copy-start(f32[768,1024]{1,0:T(8,128)} %copy-done.10) | copy-start | bytes 9437188
  (41 other events, 178.0 us)
Sparse Core Ops, SparseCore 0:
  10.2 101.7 all-gather.13
  114.1 47.4 all-gather.15
  163.8 123.4 all-gather.17
  289.2 123.1 all-gather.19
  1411.7 116.4 reduce-scatter.12
  1532.1 66.7 reduce-scatter.6
  1602.5 147.9 reduce-scatter.10
  1754.6 148.0 reduce-scatter.8
  1905.9 67.9 all-reduce.13
where the time goes:
time: 2000 us; the launch traced here: 1990 us
  matrix products  711 us (36%)
  waiting for transfers between devices  546 us (27%)
  blocking collectives  339 us (17%)
  other arithmetic  225 us (11%)
  local copies, waits for them, and re-layouts  137 us (7%)
    dot_general x24, matrix products, one_block(): jnp.einsum('bhe,lhe->hbl', query_blk[:, part], keys_all[:, part], preferr...  181 us
    dot_general x12, matrix products, one_block(): jnp.einsum('bhe,lhe->hbl', grad_blk[:, part], values_all[:, part], prefer...  167 us
    reduce_scatter x1, waiting for transfers between devices, local(): lax.psum_scatter(local_grads[7].astype(jnp.bfloat16), 'dp', scatter_dimen...  152 us
    reduce_scatter x1, waiting for transfers between devices, local(): lax.psum_scatter(local_grads[9].astype(jnp.bfloat16), 'dp', scatter_dimen...  152 us
    convert_element_type x6, other arithmetic, one_block(): d_scores = (probs_full * (d_probs - row_dot)).astype(jnp.bfloat16)  107 us
    all_to_all x1, blocking collectives, local(): lax.all_to_all(d_heads, 'seq', split_axis=0, concat_axis=2, tiled=True)  74.6 us
    reduce_scatter x1, waiting for transfers between devices, local(): lax.psum_scatter(local_grads[3].astype(jnp.bfloat16), 'dp', scatter_dimen...  68.5 us
    dot_general x12, matrix products, one_block(): jnp.einsum('hbl,lhe->bhe', probs_low, values_all[:, part], preferred_elem...  66.6 us
  transfers between devices with their start and end apart: 12, of which 7 were waited for; matrix products, arithmetic and copies ran while one was open for 19% of the time, Pallas kernels for 0%

commit v1 on v0

--- a/solution.py
+++ b/solution.py
@@ -5,6 +5,18 @@
 
 HEAD_DIM = 64
 norm_eps = 1e-05
+
+
+def doubled_up(x, axis, dim):
+    ways, here = (lax.axis_size(axis), lax.axis_index(axis))
+    grown, reach = (x, 1)
+    while reach < ways:
+        theirs = lax.ppermute(grown, axis, [(d, d ^ reach) for d in range(ways)])
+        mine_first = jnp.concatenate([grown, theirs], axis=dim)
+        theirs_first = jnp.concatenate([theirs, grown], axis=dim)
+        grown = jnp.where(here & reach == 0, mine_first, theirs_first)
+        reach = 2 * reach
+    return grown
 
 
 def shortened(array):
@@ -202,7 +214,7 @@
     queries = heads_in[:, 0, 0].reshape(length, heads_loc, HEAD_DIM)
     keys_all = heads_in[:, 1, 0].reshape(length, heads_loc, HEAD_DIM)
     values_all = heads_in[:, 2, 0].reshape(length, heads_loc, HEAD_DIM)
-    bias_row = lax.all_gather(key_bias, "seq", axis=1, tiled=True)[0]
+    bias_row = doubled_up(key_bias, "seq", 1)[0]
     context_heads, log_total = attend_forward(queries, keys_all, values_all, bias_row, score_scale)
     context = lax.all_to_all(
         shortened(context_heads.reshape(length, 1, group_width)),

time: 2000 us -> 2000 us (level)
  blocking collectives: 339 us -> 284 us
  waiting for transfers between devices: 546 us -> 598 us
    all_gather x1 -> x0, blocking collectives: 54.1 us -> none  [local(): bias_row = lax.all_gather(key_bias, 'seq', axis=1, tiled=True)[0]]
    ppermute x0 -> x2, waiting for transfers between devices: none -> 51.5 us  [doubled_up(): theirs = lax.ppermute(grown, axis, [(d, d ^ reach) for d in range(ways)])]
  transfers between devices with their start and end apart: 12 -> 14, of which waited for: 7 -> 9; matrix products, arithmetic and copies ran while one was open for 19% -> 19% of each run, Pallas kernels for 0% -> 0%
where the time goes in v1:
time: 2000 us; the launch traced here: 1990 us
  matrix products  711 us (36%)
  waiting for transfers between devices  598 us (30%)
  blocking collectives  284 us (14%)
  other arithmetic  225 us (11%)
  local copies, waits for them, and re-layouts  137 us (7%)
    dot_general x24, matrix products, one_block(): jnp.einsum('bhe,lhe->hbl', query_blk[:, part], keys_all[:, part], preferr...  181 us
    dot_general x12, matrix products, one_block(): jnp.einsum('bhe,lhe->hbl', grad_blk[:, part], values_all[:, part], prefer...  167 us
    reduce_scatter x1, waiting for transfers between devices, local(): lax.psum_scatter(local_grads[7].astype(jnp.bfloat16), 'dp', scatter_dimen...  152 us
    reduce_scatter x1, waiting for transfers between devices, local(): lax.psum_scatter(local_grads[9].astype(jnp.bfloat16), 'dp', scatter_dimen...  152 us
    convert_element_type x6, other arithmetic, one_block(): d_scores = (probs_full * (d_probs - row_dot)).astype(jnp.bfloat16)  107 us
    all_to_all x1, blocking collectives, local(): lax.all_to_all(d_heads, 'seq', split_axis=0, concat_axis=2, tiled=True)  74.6 us
    reduce_scatter x1, waiting for transfers between devices, local(): lax.psum_scatter(local_grads[3].astype(jnp.bfloat16), 'dp', scatter_dimen...  68.6 us
    dot_general x12, matrix products, one_block(): jnp.einsum('hbl,lhe->bhe', probs_low, values_all[:, part], preferred_elem...  66.4 us
  transfers between devices with their start and end apart: 14, of which 9 were waited for; matrix products, arithmetic and copies ran while one was open for 19% of the time, Pallas kernels for 0%

profile of v1, /device:TPU:0, one launch (start us, length us, event | category | flops | bytes accessed | tf_op | source)
XLA Modules:
  0.0 1988.4 jit_solution(7033304393348913157)
XLA Ops:
  9.4 22.5 %all-gather.1 = bf16[8,1,128]{2,1,0:T(2,128)(2,1)S(1)} all-gather(bf16[1,1,128]{2,1,0:T(2,128)(2,1)} %bitcast.231), channel_id=1, replica_groups=mesh['dp'=8,'seq'=4] {'dp'}, dimensions={0}, use_global_device_ids=true | all-gather | bytes 2304 | tf_op jit(solution)/shard_map/all_gather | solution.py:184
  31.9 16.7 all-gather
  48.6 63.4 %all-gather.14.cloned.1.call-done = bf16[1024,3072]{1,0:T(8,128)(2,1)} async-done(((bf16[128,3072]{1,0:T(8,128)(2,1)}), bf16[1024,3072]{1,0:T(8,128)(2,1)}) %all-gather.14.cloned.1.call-update) | async-done | bytes 6291472 | tf_op jit(solution)/shard_map/all_gather | solution.py:182
  112.0 9.0 add_convert_fusion
  121.0 9.6 reshape.383
  145.6 49.3 %collective-permute-done.1 = f32[1,1536]{1,0:T(1,128)S(1)} collective-permute-done((f32[1,1536]{1,0:T(1,128)S(1)}, f32[1,1536]{1,0:T(1,128)S(1)}, u32[]{:S(2)}, u32[]{:S(2)}) %collective-permute-start.1) | collective-permute-done | bytes 6176 | tf_op jit(solution)/shard_map/ppermute | solution.py:14
  212.5 180.4 %while.27 = (s32[]{:T(128)}, bf16[6,512,4,64]{1,3,2,0:T(8,128)(2,1)}, f32[6,4,512]{2,1,0:T(4,128)S(1)}, bf16[6,512,4,64]{1,3,2,0:T(8,128)(2,1)}, bf16[3072,4,64]...) while((s32[]{:T(128)}, bf16[6,512,4,64]{1,3,2,0:T(8,128)(2,1)}, ...), condition=%wide.region_5.6_spmd, body=%wide.region_0.5_spmd.sunk | while | flops 1686765568 | bytes 80098904 | solution.py:93
  220.1 7.9 fusion.168
  249.9 8.0 fusion.168
  280.1 7.9 fusion.168
  310.2 7.9 fusion.168
  332.6 8.2 fusion.167
  340.8 7.9 fusion.168
  370.6 7.9 fusion.168
  398.6 22.8 %reshape.414 = bf16[3072,1,256]{2,1,0:T(2,128)(2,1)} reshape(bf16[6,512,4,64]{3,2,1,0:T(4,128)(2,1)} %copy.114) | data formatting | bytes 3145728 | tf_op jit(solution)/shard_map/reshape;reshape | solution.py:220
  421.9 16.7 reduce.5
  444.8 17.5 all-gather.2
  462.3 16.8 all-gather.3
  479.2 17.5 all-gather.4
  496.7 26.0 %all-gather.5 = bf16[8,1,512]{2,1,0:T(2,128)(2,1)S(1)} all-gather(bf16[1,1,512]{2,1,0:T(2,128)(2,1)S(1)} %reshape.397), channel_id=1, replica_groups=mesh['dp'=8,'seq'=4] {'dp'}, dimensions={0}, use_global_device_ids=true | all-gather | bytes 9216 | tf_op jit(solution)/shard_map/all_gather | solution.py:190
  522.7 16.2 all-gather.6
  538.9 18.2 all-gather.7
  557.1 16.2 all-gather.8
  585.4 39.4 %multiply_convert_fusion.2 = (bf16[768,4096]{1,0:T(8,128)(2,1)}, f32[768,4096]{1,0:T(8,128)}, f32[768,4096]{1,0:T(8,128)}) fusion(f32[4096]{0:T(1024)S(1)} %bitcast.222, bf16[1024,4096]{1,0:T(8,128)(2,1)} %all-gather.18.cloned.1.call-done, f32[768,1024]{1,0:T(8,128)S(1)} %get-tuple-element.410, f32[1024]{0:T(1024)S(1)} %bitcast.226, ...), kind=kOutput, calls=%fused_computation.100 | convolution fusion | flops 6654001152 | bytes 43022336 | tf_op jit(solution)/shard_map/dot_general | solution.py:42
  624.8 11.7 fusion.105
  641.8 21.7 %fusion.106 = (bf16[4096]{0:T(1024)(128)(2,1)}, bf16[768,4096]{1,0:T(8,128)(2,1)}) fusion(f32[768,4096]{1,0:T(8,128)} %get-tuple-element.392, bf16[4096,1024]{1,0:T(8,128)(2,1)} %all-gather.20.cloned.1.call-done, f32[768,1024]{1,0:T(8,128)} %get-tuple-element.390, f32[768]{0:T(1024)S(1)} %negate_multiply_fusion.2, f32[768,4096]{1,0:T(8,128)} %get-tuple-element.411, ...), kind=kOutput, calls=%fused_computation.170 | convolution fusion | flops 6494351360 | bytes 43019264 | tf_op jit(solution)/shard_map/dot_general | solution.py:52
  663.5 13.4 multiply_reduce_fusion.2
  686.7 20.0 %all-to-all-done.2 = bf16[768,4,256]{0,2,1:T(8,128)(2,1)S(1)} async-done(((bf16[768,4,256]{0,2,1:T(8,128)(2,1)}), bf16[768,4,256]{0,2,1:T(8,128)(2,1)S(1)}, u32[]{:S(2)}, u32[]{:S(2)}) %all-to-all-start.2) | async-done | bytes 1572896 | tf_op jit(solution)/shard_map/all_to_all | solution.py:258
  716.5 569.3 %while.28 = (s32[]{:T(128)}, f32[3072,4,64]{0,2,1:T(8,128)}, f32[3072,4,64]{0,2,1:T(8,128)}, bf16[6,512,4,64]{1,3,2,0:T(8,128)(2,1)}, bf16[6,512,4,64]{1,3,2,0:T...) while((s32[]{:T(128)}, f32[3072,4,64]{0,2,1:T(8,128)}, ...), condition=%wide.region_17.18_spmd.clone, body=%wide.region_14.17_spmd.clone.sunk | while | flops 4127193088 | bytes 341160832 | solution.py:156
  731.3 7.7 fusion.192
  739.7 20.2 %multiply_reduce_fusion.7 = (f32[2,512]{1,0:T(2,128)S(1)}, f32[2,512]{1,0:T(2,128)S(1)}, f32[2,512,3072]{2,1,0:T(8,128)}) fusion(f32[2,512,3072]{2,1,0:T(8,128)} %fusion.191, f32[2,512]{1,0:T(2,128)S(1)} %get-tuple-element.546, f32[3072]{0:T(1024)S(1)} %bitcast.204, f32[2,512,3072]{2,1,0:T(8,128)} %fusion.192, f32[2,512]{1,0:T(2,128)S(1)} %get-tuple-element.547, ...), kind=kOutput, calls=%fused_computation.39.clone.1 | convolution fusion | flops 434108416 | bytes 51409408 | tf_op jit(solution)/shard_map/while/body/eval_jaxpr/bhe,lhe->hbl/dot_general | solution.py:123
  759.9 17.9 multiply_convert_fusion.4
  824.5 7.7 fusion.192
  833.0 20.1 %multiply_reduce_fusion.7 = (f32[2,512]{1,0:T(2,128)S(1)}, f32[2,512]{1,0:T(2,128)S(1)}, f32[2,512,3072]{2,1,0:T(8,128)}) fusion(f32[2,512,3072]{2,1,0:T(8,128)} %fusion.191, f32[2,512]{1,0:T(2,128)S(1)} %get-tuple-element.546, f32[3072]{0:T(1024)S(1)} %bitcast.204, f32[2,512,3072]{2,1,0:T(8,128)} %fusion.192, f32[2,512]{1,0:T(2,128)S(1)} %get-tuple-element.547, ...), kind=kOutput, calls=%fused_computation.39.clone.1 | convolution fusion | flops 434108416 | bytes 51409408 | tf_op jit(solution)/shard_map/while/body/eval_jaxpr/bhe,lhe->hbl/dot_general | solution.py:123
  853.1 17.9 multiply_convert_fusion.4
  896.2 8.8 maximum_add_fusion.3
  919.6 7.7 fusion.192
  928.0 20.2 %multiply_reduce_fusion.7 = (f32[2,512]{1,0:T(2,128)S(1)}, f32[2,512]{1,0:T(2,128)S(1)}, f32[2,512,3072]{2,1,0:T(8,128)}) fusion(f32[2,512,3072]{2,1,0:T(8,128)} %fusion.191, f32[2,512]{1,0:T(2,128)S(1)} %get-tuple-element.546, f32[3072]{0:T(1024)S(1)} %bitcast.204, f32[2,512,3072]{2,1,0:T(8,128)} %fusion.192, f32[2,512]{1,0:T(2,128)S(1)} %get-tuple-element.547, ...), kind=kOutput, calls=%fused_computation.39.clone.1 | convolution fusion | flops 434108416 | bytes 51409408 | tf_op jit(solution)/shard_map/while/body/eval_jaxpr/bhe,lhe->hbl/dot_general | solution.py:123
  948.2 17.9 multiply_convert_fusion.4
  991.4 8.8 maximum_add_fusion.3
  1014.7 7.7 fusion.192
  1023.2 20.2 %multiply_reduce_fusion.7 = (f32[2,512]{1,0:T(2,128)S(1)}, f32[2,512]{1,0:T(2,128)S(1)}, f32[2,512,3072]{2,1,0:T(8,128)}) fusion(f32[2,512,3072]{2,1,0:T(8,128)} %fusion.191, f32[2,512]{1,0:T(2,128)S(1)} %get-tuple-element.546, f32[3072]{0:T(1024)S(1)} %bitcast.204, f32[2,512,3072]{2,1,0:T(8,128)} %fusion.192, f32[2,512]{1,0:T(2,128)S(1)} %get-tuple-element.547, ...), kind=kOutput, calls=%fused_computation.39.clone.1 | convolution fusion | flops 434108416 | bytes 51409408 | tf_op jit(solution)/shard_map/while/body/eval_jaxpr/bhe,lhe->hbl/dot_general | solution.py:123
  1043.4 17.9 multiply_convert_fusion.4
  1086.5 8.8 maximum_add_fusion.3
  1109.8 7.7 fusion.192
  1118.3 20.2 %multiply_reduce_fusion.7 = (f32[2,512]{1,0:T(2,128)S(1)}, f32[2,512]{1,0:T(2,128)S(1)}, f32[2,512,3072]{2,1,0:T(8,128)}) fusion(f32[2,512,3072]{2,1,0:T(8,128)} %fusion.191, f32[2,512]{1,0:T(2,128)S(1)} %get-tuple-element.546, f32[3072]{0:T(1024)S(1)} %bitcast.204, f32[2,512,3072]{2,1,0:T(8,128)} %fusion.192, f32[2,512]{1,0:T(2,128)S(1)} %get-tuple-element.547, ...), kind=kOutput, calls=%fused_computation.39.clone.1 | convolution fusion | flops 434108416 | bytes 51409408 | tf_op jit(solution)/shard_map/while/body/eval_jaxpr/bhe,lhe->hbl/dot_general | solution.py:123
  1138.5 17.9 multiply_convert_fusion.4
  1181.6 8.8 maximum_add_fusion.3
  1213.4 20.2 %multiply_reduce_fusion.7 = (f32[2,512]{1,0:T(2,128)S(1)}, f32[2,512]{1,0:T(2,128)S(1)}, f32[2,512,3072]{2,1,0:T(8,128)}) fusion(f32[2,512,3072]{2,1,0:T(8,128)} %fusion.191, f32[2,512]{1,0:T(2,128)S(1)} %get-tuple-element.546, f32[3072]{0:T(1024)S(1)} %bitcast.204, f32[2,512,3072]{2,1,0:T(8,128)} %fusion.192, f32[2,512]{1,0:T(2,128)S(1)} %get-tuple-element.547, ...), kind=kOutput, calls=%fused_computation.39.clone.1 | convolution fusion | flops 434108416 | bytes 51409408 | tf_op jit(solution)/shard_map/while/body/eval_jaxpr/bhe,lhe->hbl/dot_general | solution.py:123
  1233.6 17.9 multiply_convert_fusion.4
  1276.7 8.8 maximum_add_fusion.3
  1298.8 10.1 copy.110
  1309.0 74.6 %all_to_all.63 = bf16[3072,3,1,256]{3,1,2,0:T(4,128)(2,1)S(1)} all-to-all(bf16[3072,3,1,256]{3,1,2,0:T(4,128)(2,1)} %copy.110), channel_id=1, replica_groups=mesh['dp'=8,'seq'=4] {'seq'}, dimensions={0} | all-to-all | bytes 9437184 | tf_op jit(solution)/shard_map/all_to_all | solution.py:279
  1393.2 9.4 convert_bitcast_fusion
  1402.6 8.6 copy.116
  1417.8 12.5 convolution_convert_fusion
  1432.2 12.3 convolution_convert_fusion.1
  1453.6 36.6 %all-reduce.9 = (bf16[1024]{0:T(1024)(128)(2,1)S(1)}, bf16[1024]{0:T(1024)(128)(2,1)S(1)}, bf16[1024]{0:T(1024)(128)(2,1)S(1)}, bf16[1024]{0:T(1024)(128)(2,1)S(...) all-reduce(bf16[1024]{0:T(1024)(128)(2,1)S(1)} %get-tuple-element.3, ...), channel_id=3, replica_groups=mesh['dp'=8,'seq'=4] {'dp'}, use_global_device_ids=true, to_apply=%region_21.22.clone | all-reduce | flops 12288 | bytes 49152
  1501.2 26.6 %reduce-scatter.13.cloned.1.call-done = bf16[128,3072]{1,0:T(8,128)(2,1)} async-done(((bf16[1024,3072]{1,0:T(8,128)(2,1)}), bf16[128,3072]{1,0:T(8,128)(2,1)}) %reduce-scatter.13.cloned.1.call-update) | async-done | bytes 786448
  1530.1 68.6 %reduce-scatter.7.cloned.1.call-done = bf16[128,1024]{1,0:T(8,128)(2,1)} async-done(((bf16[1024,1024]{1,0:T(8,128)(2,1)}), bf16[128,1024]{1,0:T(8,128)(2,1)}) %reduce-scatter.7.cloned.1.call-update) | async-done | bytes 262160 | tf_op jit(solution)/shard_map/reduce_scatter | solution.py:311
  1598.7 151.7 %reduce-scatter.11.cloned.1.call-done = bf16[512,1024]{1,0:T(8,128)(2,1)} async-done(((bf16[4096,1024]{1,0:T(8,128)(2,1)}), bf16[512,1024]{1,0:T(8,128)(2,1)}) %reduce-scatter.11.cloned.1.call-update) | async-done | bytes 1048592 | tf_op jit(solution)/shard_map/reduce_scatter | solution.py:329
  1750.5 152.1 %reduce-scatter.9.cloned.1.call-done = bf16[128,4096]{1,0:T(8,128)(2,1)} async-done(((bf16[1024,4096]{1,0:T(8,128)(2,1)}), bf16[128,4096]{1,0:T(8,128)(2,1)}) %reduce-scatter.9.cloned.1.call-update) | async-done | bytes 1048592 | tf_op jit(solution)/shard_map/reduce_scatter | solution.py:323
  1902.6 9.8 add_add_fusion.4
  1912.5 61.3 %all-reduce.14.cloned.1.call-done = (bf16[128,3072]{0,1:T(8,128)(2,1)}, bf16[128,1024]{1,0:T(8,128)(2,1)}, bf16[128,4096]{1,0:T(8,128)(2,1)}, bf16[512,1024]{1,0:T(8,128)(2,1)}) async-done(((bf16[128,3072]{0,1:T(8,128)(2,1)}, bf16[128,1024]{1,0:T(8,128)(2,1)}, bf16[128,4096]{1,0:T(8,128)(2,1)}, bf16[512,1024]{1,0:T(8,128)(2,1)}), (bf16[128,3072]{0,1:T(8,128)(2,1)}, bf16[128,1024]{1,0:T(8,128)(2,1)}, ...) | async-done | bytes 3145744 | tf_op jit(solution)/shard_map/psum | solution.py:343
  (422 shorter events, 525.4 us)
Async XLA Ops:
  7.2 104.8 %all-gather.14.cloned.1.call-start = ((), (), s32[]{:S(2)}) async-start(), calls=%async_computation.8 | async-start | bytes 7077888 | tf_op jit(solution)/shard_map/all_gather | solution.py:182
  7.9 572.4 %all-gather.16.cloned.1.call-start = ((), (), s32[]{:S(2)}) async-start(), calls=%async_computation.9 | async-start | bytes 2359296 | tf_op jit(solution)/shard_map/all_gather | solution.py:185
  8.7 576.7 %all-gather.18.cloned.1.call-start = ((), (), s32[]{:S(2)}) async-start(), calls=%async_computation.10 | async-start | bytes 9437184 | tf_op jit(solution)/shard_map/all_gather | solution.py:189
  135.9 59.1 %all-to-all-start = ((bf16[768,3,4,256]{3,0,1,2:T(8,128)(2,1)}), bf16[768,3,4,256]{3,0,1,2:T(8,128)(2,1)}, u32[]{:S(2)}, u32[]{:S(2)}) async-start(bf16[768,3,4,256]{3,0,1,2:T(8,128)(2,1)} %copy.96), calls=%async_computation | async-start | bytes 9437184 | tf_op jit(solution)/shard_map/all_to_all | solution.py:212
  141.1 483.7 %all-gather.20.cloned.1.call-start = ((), (), s32[]{:S(2)}) async-start(), calls=%async_computation.11 | async-start | bytes 9437184 | tf_op jit(solution)/shard_map/all_gather | solution.py:191
  141.1 2.7 collective-permute-start
  143.9 51.1 %collective-permute-start.1 = (f32[1,1536]{1,0:T(1,128)S(1)}, f32[1,1536]{1,0:T(1,128)S(1)}, u32[]{:S(2)}, u32[]{:S(2)}) collective-permute-start(f32[1,1536]{1,0:T(1,128)S(1)} %broadcast_select_fusion.1), channel_id=1, source_target_pairs={{0,2},{1,3},{2,0},{3,1},{4,6},{5,7},{6,4},{7,5},{8,10},{9,11},{10,... | collective-permute-start | bytes 18440 | tf_op jit(solution)/shard_map/ppermute | solution.py:14
  392.9 28.4 %copy-start.1 = (bf16[3072,4,64]{0,2,1:T(8,128)(2,1)}, bf16[3072,4,64]{0,2,1:T(8,128)(2,1)S(1)}, u32[]{:S(2)}) copy-start(bf16[3072,4,64]{0,2,1:T(8,128)(2,1)S(1)} %get-tuple-element.634) | copy-start | bytes 4718596
  392.9 28.4 %copy-start.14 = (f32[1,3072]{1,0:T(1,128)}, f32[1,3072]{1,0:T(1,128)S(1)}, u32[]{:S(2)}) copy-start(f32[1,3072]{1,0:T(1,128)S(1)} %get-tuple-element.653) | copy-start | bytes 36868
  392.9 28.4 %copy-start.21 = (f32[6,4,512]{2,1,0:T(4,128)}, f32[6,4,512]{2,1,0:T(4,128)S(1)}, u32[]{:S(2)}) copy-start(f32[6,4,512]{2,1,0:T(4,128)S(1)} %get-tuple-element.586) | copy-start | bytes 147460
  421.9 22.9 %copy-start.38 = (bf16[128]{0:T(256)(128)(2,1)S(1)}, bf16[128]{0:T(256)(128)(2,1)}, u32[]{:S(2)}) copy-start(bf16[128]{0:T(256)(128)(2,1)} %param.26) | copy-start | bytes 772
  421.9 40.5 %copy-start.39 = (bf16[128]{0:T(256)(128)(2,1)S(1)}, bf16[128]{0:T(256)(128)(2,1)}, u32[]{:S(2)}) copy-start(bf16[128]{0:T(256)(128)(2,1)} %param.27) | copy-start | bytes 772
  421.9 57.3 %copy-start.40 = (bf16[128]{0:T(256)(128)(2,1)S(1)}, bf16[128]{0:T(256)(128)(2,1)}, u32[]{:S(2)}) copy-start(bf16[128]{0:T(256)(128)(2,1)} %param.28) | copy-start | bytes 772
  421.9 74.8 %copy-start.37 = (bf16[512]{0:T(512)(128)(2,1)S(1)}, bf16[512]{0:T(512)(128)(2,1)}, u32[]{:S(2)}) copy-start(bf16[512]{0:T(512)(128)(2,1)} %param.30) | copy-start | bytes 3076
  421.9 100.9 %copy-start.41 = (bf16[128]{0:T(256)(128)(2,1)S(1)}, bf16[128]{0:T(256)(128)(2,1)}, u32[]{:S(2)}) copy-start(bf16[128]{0:T(256)(128)(2,1)} %param.32) | copy-start | bytes 772
  421.9 117.0 %copy-start.42 = (bf16[128]{0:T(256)(128)(2,1)S(1)}, bf16[128]{0:T(256)(128)(2,1)}, u32[]{:S(2)}) copy-start(bf16[128]{0:T(256)(128)(2,1)} %param.33) | copy-start | bytes 772
  421.9 135.2 %copy-start.43 = (bf16[128]{0:T(256)(128)(2,1)S(1)}, bf16[128]{0:T(256)(128)(2,1)}, u32[]{:S(2)}) copy-start(bf16[128]{0:T(256)(128)(2,1)} %param.34) | copy-start | bytes 772
  440.4 132.8 %all-to-all-start.1 = ((bf16[4,2,98304]{2,1,0:T(2,128)(2,1)}), bf16[4,2,98304]{2,1,0:T(2,128)(2,1)}, u32[]{:S(2)}, u32[]{:S(2)}) async-start(bf16[4,2,98304]{2,1,0:T(2,128)(2,1)} %reshape.429), calls=%async_computation.1 | async-start | bytes 3145728 | tf_op jit(solution)/shard_map/all_to_all | solution.py:219
  479.1 197.8 %copy-start.24 = (f32[8,1,128]{2,1,0:T(1,128)}, f32[8,1,128]{2,1,0:T(1,128)S(1)}, u32[]{:S(2)}) copy-start(f32[8,1,128]{2,1,0:T(1,128)S(1)} %convert_element_type.240) | copy-start | bytes 12292
  496.7 128.1 %copy-start.33 = (f32[8,1,128]{2,1,0:T(1,128)}, f32[8,1,128]{2,1,0:T(1,128)S(1)}, u32[]{:S(2)}) copy-start(f32[8,1,128]{2,1,0:T(1,128)S(1)} %convert_element_type.241) | copy-start | bytes 12292
  584.9 92.1 %copy-start.8 = (f32[768,1024]{1,0:T(8,128)}, f32[768,1024]{1,0:T(8,128)S(1)}, u32[]{:S(2)}) copy-start(f32[768,1024]{1,0:T(8,128)S(1)} %get-tuple-element.410) | copy-start | bytes 9437188
  584.9 92.0 %copy-start.19 = (f32[768]{0:T(1024)}, f32[768]{0:T(1024)S(1)}, u32[]{:S(2)}) copy-start(f32[768]{0:T(1024)S(1)} %broadcast_multiply_fusion.1) | copy-start | bytes 9220
  585.3 91.6 %copy-start.26 = (f32[768]{0:T(1024)}, f32[768]{0:T(1024)S(1)}, u32[]{:S(2)}) copy-start(f32[768]{0:T(1024)S(1)} %fusion.94) | copy-start | bytes 9220
  624.8 12.2 copy-start.6
  641.8 21.7 %copy-start.28 = (f32[768]{0:T(1024)}, f32[768]{0:T(1024)S(1)}, u32[]{:S(2)}) copy-start(f32[768]{0:T(1024)S(1)} %negate_multiply_fusion.2) | copy-start | bytes 9220
  683.0 23.6 %all-to-all-start.2 = ((bf16[768,4,256]{0,2,1:T(8,128)(2,1)}), bf16[768,4,256]{0,2,1:T(8,128)(2,1)S(1)}, u32[]{:S(2)}, u32[]{:S(2)}) async-start(bf16[768,4,256]{0,2,1:T(8,128)(2,1)} %bitcast.33), calls=%async_computation.2 | async-start | bytes 3145728 | tf_op jit(solution)/shard_map/all_to_all | solution.py:258
  686.6 841.2 %reduce-scatter.13.cloned.1.call-start = ((), (), s32[]{:S(2)}) async-start(), calls=%async_computation.15 | async-start | bytes 7077888
  706.7 9.9 copy-start.2
  706.7 9.9 copy-start.15
  777.8 15.6 slice-start.3
  781.7 11.7 slice-start.4
  785.8 7.6 slice-start.5
  790.0 8.3 slice-start
  871.0 15.6 slice-start.3
  874.9 11.7 slice-start.4
  879.0 7.6 slice-start.5
  883.2 8.3 slice-start
  896.2 8.8 copy-start.3
  966.1 15.6 slice-start.3
  970.0 11.7 slice-start.4
  974.1 7.6 slice-start.5
  978.3 8.3 slice-start
  991.4 8.8 copy-start.3
  1061.3 15.6 slice-start.3
  1065.2 11.7 slice-start.4
  1069.2 7.6 slice-start.5
  1073.4 8.3 slice-start
  1086.5 8.8 copy-start.3
  1156.4 15.6 slice-start.3
  1160.3 11.7 slice-start.4
  1164.3 7.6 slice-start.5
  1168.5 8.3 slice-start
  1181.6 8.8 copy-start.3
  1251.5 15.6 slice-start.3
  1255.4 11.7 slice-start.4
  1259.4 7.6 slice-start.5
  1263.6 8.3 slice-start
  1276.7 8.8 copy-start.3
  1285.9 8.2 copy-start.4
  1411.3 187.5 %reduce-scatter.7.cloned.1.call-start = ((), (), s32[]{:S(2)}) async-start(), calls=%async_computation.12 | async-start | bytes 2359296 | tf_op jit(solution)/shard_map/reduce_scatter | solution.py:311
  1417.7 332.7 %reduce-scatter.11.cloned.1.call-start = ((), (), s32[]{:S(2)}) async-start(), calls=%async_computation.14 | async-start | bytes 9437184 | tf_op jit(solution)/shard_map/reduce_scatter | solution.py:329
  1430.3 472.3 %reduce-scatter.9.cloned.1.call-start = ((), (), s32[]{:S(2)}) async-start(), calls=%async_computation.13 | async-start | bytes 9437184 | tf_op jit(solution)/shard_map/reduce_scatter | solution.py:323
  1444.6 529.2 %all-reduce.14.cloned.1.call-start = ((), (), s32[]{:S(2)}) async-start(), calls=%async_computation.16 | async-start | bytes 6291456 | tf_op jit(solution)/shard_map/psum | solution.py:343
  1451.0 451.6 %copy-start.12 = (f32[768,1024]{1,0:T(8,128)S(1)}, f32[768,1024]{1,0:T(8,128)}, u32[]{:S(2)}) copy-start(f32[768,1024]{1,0:T(8,128)} %copy-done.10) | copy-start | bytes 9437188
  (43 other events, 191.7 us)
Sparse Core Ops, SparseCore 0:
  10.2 101.7 all-gather.13
  114.1 47.4 all-gather.15
  163.8 123.4 all-gather.17
  289.2 123.1 all-gather.19
  1411.4 116.3 reduce-scatter.12
  1531.8 66.9 reduce-scatter.6
  1602.4 148.0 reduce-scatter.10
  1754.5 148.0 reduce-scatter.8
  1905.8 67.9 all-reduce.13
